TPU v7x, 32 devices: a whole 2x2x4 slice. The times are simulated.
32 devices in a mesh: dom: 32 (over z, y, x, core).
Axes of the slice: x: 2, y: 2, z: 4, core: 2. Of those that a mesh axis runs over, the one named last changes fastest.
Arguments:
- embeddings: float32 [16384, 256], P('dom'), may hold values from -1.75 to 1.75
- emb_state: float32 [16384], P('dom'), may hold values from 0.001 to 0.1
- relations: float32 [64, 256], replicated, may hold values from -6 to 6
- rel_state: float32 [64, 256], replicated, may hold values from 0.001 to 0.1
- matching: int32 [2], replicated, may hold values from 1 to 31
- src_index: int32 [2, 8192], P(None, 'dom'), may hold values from 0 to 511
- dst_index: int32 [2, 8192], P(None, 'dom'), may hold values from 0 to 511
- rel_index: int32 [2, 8192], P(None, 'dom'), may hold values from 0 to 63
- neg_index: int32 [2, 32768], P(None, 'dom'), may hold values from 0 to 511
- counts: int32 [2, 32], P(None, 'dom'), may hold values from 1 to 256, 4096 in all within a row
Outputs:
- new_embeddings: float32 [16384, 256], P('dom')
- new_emb_state: float32 [16384], P('dom')
- new_relations: float32 [64, 256], replicated
- new_rel_state: float32 [64, 256], replicated
Inputs may be any that keep to these rules, and one draw needn't show every extreme that they name: Round k pairs partition p with partition p XOR matching[k]. `counts`: some bucket of each round is full.
All inputs are finite; a program needn't handle non-finite values. No bound on the sum of `counts` on one device may be relied on, other than what follows from the above.
Results may differ from a plain program's by a relative error of at most 0.0029.
Values may be sent and summed in bfloat16 or wider, within the bound.
A program may use at most 64 MiB of HBM per device.

v0:
```python
import jax
import jax.numpy as jnp
from jax import lax
from jax.sharding import PartitionSpec as P

GROUP = 256
ROUNDS = 2


LEARN_RATE = 0.1
EPSILON = 1e-06


def as_sent(array):

    def short(part):
        return part.astype(jnp.bfloat16) if part.dtype == jnp.float32 else part

    return jax.tree.map(short, array)


def partner(value, axis, stride):
    mask = 2**stride
    pairs = [(source, source ^ mask) for source in range(lax.axis_size(axis))]
    return lax.ppermute(value, axis, pairs)


def complex_times(values, factor):
    half_width = values.shape[-1] // 2
    val_real, val_imag = (values[..., :half_width], values[..., half_width:])
    fac_real, fac_imag = (factor[..., :half_width], factor[..., half_width:])
    return jnp.concatenate(
        [val_real * fac_real - val_imag * fac_imag, val_real * fac_imag + val_imag * fac_real],
        axis=-1,
    )


def conj_times(values, factor):
    half_width = values.shape[-1] // 2
    val_real, val_imag = (values[..., :half_width], values[..., half_width:])
    fac_real, fac_imag = (factor[..., :half_width], factor[..., half_width:])
    return jnp.concatenate(
        [val_real * fac_real + val_imag * fac_imag, -val_real * fac_imag + val_imag * fac_real],
        axis=-1,
    )


def group_terms(src_bf, dst_bf, neg_bf, rel_rows, live_edge):
    source = src_bf.astype(jnp.float32)
    target = dst_bf.astype(jnp.float32)
    query = complex_times(source, rel_rows)
    positive = jnp.sum(query * target, axis=-1)
    query_bf = query.astype(jnp.bfloat16)
    scores = lax.dot_general(
        query_bf, neg_bf, (((1,), (1,)), ((), ())), preferred_element_type=jnp.float32
    )
    grad_pos = -jax.nn.sigmoid(-positive) * live_edge
    grad_score = (jax.nn.sigmoid(scores) * (live_edge / neg_bf.shape[0])[:, None]).astype(
        jnp.bfloat16
    )
    grad_query = grad_pos[:, None] * target + jnp.dot(
        grad_score, neg_bf, preferred_element_type=jnp.float32
    )
    grad_dst = grad_pos[:, None] * query
    grad_neg = lax.dot_general(
        grad_score, query_bf, (((0,), (0,)), ((), ())), preferred_element_type=jnp.float32
    )
    return (conj_times(grad_query, rel_rows), grad_dst, grad_neg, conj_times(grad_query, source))


def row_adagrad(params, state, grad):
    new_state = state + jnp.mean(grad * grad, axis=-1)
    return (params - LEARN_RATE * grad / (jnp.sqrt(new_state) + EPSILON)[:, None], new_state)


def plain_adagrad(params, state, grad):
    new_state = state + grad * grad
    return (params - LEARN_RATE * grad / (jnp.sqrt(new_state) + EPSILON), new_state)


def on_device(
    embeddings,
    emb_state,
    relations,
    rel_state,
    matching,
    src_index,
    dst_index,
    rel_index,
    neg_index,
    counts,
):
    bit_count = lax.axis_size("dom").bit_length() - 1
    bit_list = list(range(bit_count))
    rel_count = relations.shape[0]
    edge_slots = src_index.shape[1]
    positions = jnp.arange(GROUP, dtype=jnp.int32)
    rel_numbers = jnp.arange(rel_count, dtype=jnp.int32)
    for round_id in range(ROUNDS):
        xor_mask = matching[round_id]
        outgoing = (
            jnp.take(embeddings, src_index[round_id], axis=0).astype(jnp.bfloat16),
            dst_index[round_id],
            rel_index[round_id],
            neg_index[round_id],
            counts[round_id],
        )
        payload = outgoing
        for send_bit_number in bit_list:
            send_chosen = jnp.right_shift(xor_mask, send_bit_number) % 2 == 1
            send_received = jax.tree.map(
                lambda part, own: part.astype(own.dtype),
                partner(as_sent(payload), "dom", send_bit_number),
                payload,
            )
            payload = tuple(
                (
                    jnp.where(send_chosen, new_part, old_part)
                    for old_part, new_part in zip(payload, send_received)
                )
            )
        rows_in, dst_in, rel_in, neg_in, count_in = payload
        edge_total = count_in[0]
        group_total = (edge_total + GROUP - 1) // GROUP

        def group_step(group_id, carry):
            grad_local, grad_source, grad_rel = carry
            first_edge = group_id * GROUP
            live_edge = (first_edge + positions < edge_total).astype(jnp.float32)
            dst_bf = jnp.take(embeddings, dst_in, axis=0).astype(jnp.bfloat16)
            neg_bf = jnp.take(embeddings, neg_in, axis=0).astype(jnp.bfloat16)
            selector = (rel_in[:, None] == rel_numbers[None, :]).astype(jnp.float32)
            rel_rows = jnp.dot(
                selector,
                relations,
                precision=lax.Precision.HIGHEST,
                preferred_element_type=jnp.float32,
            )
            grad_src, grad_dst, grad_neg, grad_relation = group_terms(
                rows_in, dst_bf, neg_bf, rel_rows, live_edge
            )
            grad_local = grad_local.at[dst_in].add(grad_dst).at[neg_in].add(grad_neg)
            grad_source = grad_src
            grad_rel = grad_rel + lax.dot_general(
                selector,
                grad_relation,
                (((0,), (0,)), ((), ())),
                precision=lax.Precision.HIGHEST,
                preferred_element_type=jnp.float32,
            )
            return (grad_local, grad_source, grad_rel)

        start_carry = (
            jnp.zeros(embeddings.shape, jnp.float32),
            jnp.zeros((edge_slots, embeddings.shape[1]), jnp.float32),
            jnp.zeros(relations.shape, jnp.float32),
        )
        grad_local, grad_source, grad_rel = lax.fori_loop(0, group_total, group_step, start_carry)
        grads = grad_source
        for bit_number in bit_list:
            chosen = jnp.right_shift(xor_mask, bit_number) % 2 == 1
            received = partner(grads, "dom", bit_number)
            grads = jnp.where(chosen, received, grads)
        grad_local = grad_local.at[src_index[round_id]].add(grads)
        embeddings, emb_state = row_adagrad(embeddings, emb_state, grad_local)
        grad_total = lax.psum(grad_rel, "dom")
        relations, rel_state = plain_adagrad(relations, rel_state, grad_total)
    return (embeddings, emb_state, relations, rel_state)


def solution(mesh):
    return jax.shard_map(
        on_device,
        mesh=mesh,
        in_specs=(
            P("dom", None),
            P("dom"),
            P(),
            P(),
            P(),
            P(None, "dom"),
            P(None, "dom"),
            P(None, "dom"),
            P(None, "dom"),
            P(None, "dom"),
        ),
        out_specs=(P("dom", None), P("dom"), P(), P()),
        check_vma=False,
    )
```

profile of v0, /device:TPU:0, one launch (start us, length us, event | category | flops | bytes accessed | tf_op | source)
XLA Modules:
  0.0 472.8 jit_solution(10451843377558523267)
XLA Ops:
  22.7 4.3 collective-permute-start.1
  31.8 2.8 collective-permute-start.2
  35.5 2.8 collective-permute-start.32
  39.0 2.9 collective-permute-start.3
  42.6 2.9 collective-permute-start.33
  46.2 4.0 collective-permute-start.4
  50.8 3.7 collective-permute-start.34
  76.9 2.3 collective-permute-start.9
  81.4 2.3 collective-permute-start.19
  95.0 2.6 collective-permute-done.12
  99.2 2.3 collective-permute-start.24
  102.7 2.4 collective-permute-start.14
  105.1 4.9 %collective-permute-done.14 = bf16[256,256]{0,1:T(8,128)(2,1)S(1)} collective-permute-done((bf16[256,256]{0,1:T(8,128)(2,1)S(1)}, bf16[256,256]{0,1:T(8,128)(2,1)S(1)}, u32[]{:S(2)}, u32[]{:S(2)}) %collective-permute-start.14) | collective-permute-done | bytes 131104 | tf_op jit(solution)/shard_map/ppermute | solution.py:25
  110.9 16.1 %while.40 = (s32[]{:T(128)}, f32[512,256]{1,0:T(8,128)S(1)}, f32[256,256]{0,1:T(8,128)}, f32[64,256]{1,0:T(8,128)S(1)}, s32[]{:T(128)}, /*index=5*/s32[256]{0:T(...) while((s32[]{:T(128)}, f32[512,256]{1,0:T(8,128)S(1)}, ...), condition=%wide.region_4.8_spmd.clone, body=%wide.region_1.7_spmd.clone.sunk | while | flops 507231744 | bytes 14395561 | solution.py:158
  111.4 3.9 gather_fusion
  120.5 6.3 %scatter_fusion.1 = f32[512,256]{1,0:T(8,128)S(1)} fusion(f32[512,256]{1,0:T(8,128)S(1)} %scatter_fusion, s32[1024]{0:T(1024)S(1)} %bitcast.84, f32[1024,256]{1,0:T(8,128)S(1)} %fusion.119), kind=kCustom, calls=%fused_computation.7.clone.clone.1 | custom fusion | flops 262144 | bytes 3149824 | tf_op jit(solution)/shard_map/while/body/scatter-add | solution.py:142
  134.5 2.9 collective-permute-done.26
  139.5 5.2 %collective-permute-done.27 = f32[256,256]{0,1:T(8,128)S(1)} collective-permute-done((f32[256,256]{0,1:T(8,128)S(1)}, f32[256,256]{0,1:T(8,128)S(1)}, u32[]{:S(2)}, u32[]{:S(2)}) %collective-permute-start.27) | collective-permute-done | bytes 262176 | tf_op jit(solution)/shard_map/ppermute | solution.py:25
  145.3 5.9 %collective-permute-done.28 = f32[256,256]{0,1:T(8,128)S(1)} collective-permute-done((f32[256,256]{0,1:T(8,128)S(1)}, f32[256,256]{0,1:T(8,128)S(1)}, u32[]{:S(2)}, u32[]{:S(2)}) %collective-permute-start.28) | collective-permute-done | bytes 262176 | tf_op jit(solution)/shard_map/ppermute | solution.py:25
  151.2 3.7 collective-permute-start.29
  155.9 7.7 %collective-permute-done.29 = f32[256,256]{0,1:T(8,128)S(1)} collective-permute-done((f32[256,256]{0,1:T(8,128)S(1)}, f32[256,256]{0,1:T(8,128)S(1)}, u32[]{:S(2)}, u32[]{:S(2)}) %collective-permute-start.29) | collective-permute-done | bytes 262176 | tf_op jit(solution)/shard_map/ppermute | solution.py:25
  176.2 3.8 collective-permute-done.42
  180.9 112.3 %all-reduce.3.cloned.1.call-done = f32[64,256]{1,0:T(8,128)} async-done(((f32[64,256]{1,0:T(8,128)}), f32[64,256]{1,0:T(8,128)}) %all-reduce.3.cloned.1.call-update) | async-done | bytes 65552 | tf_op jit(solution)/shard_map/psum | solution.py:166
  294.7 3.2 collective-permute-start.44
  300.1 4.7 %collective-permute-done.44 = bf16[256,256]{0,1:T(8,128)(2,1)S(1)} collective-permute-done((bf16[256,256]{0,1:T(8,128)(2,1)S(1)}, bf16[256,256]{0,1:T(8,128)(2,1)S(1)}, u32[]{:S(2)}, u32[]{:S(2)}) %collective-permute-start.44) | collective-permute-done | bytes 131104 | tf_op jit(solution)/shard_map/ppermute | solution.py:25
  305.8 16.7 %while.41 = (s32[]{:T(128)}, f32[512,256]{1,0:T(8,128)S(1)}, f32[256,256]{0,1:T(8,128)}, f32[64,256]{1,0:T(8,128)S(1)}, s32[]{:T(128)}, /*index=5*/s32[256]{0:T(...) while((s32[]{:T(128)}, f32[512,256]{1,0:T(8,128)S(1)}, ...), condition=%wide.region_12.16_spmd.clone, body=%wide.region_9.15_spmd.clone.sunk | while | flops 507231744 | bytes 14395561 | solution.py:158
  307.1 3.9 gather_fusion.1
  316.2 6.3 %scatter_fusion.3 = f32[512,256]{1,0:T(8,128)S(1)} fusion(f32[512,256]{1,0:T(8,128)S(1)} %scatter_fusion.2, s32[1024]{0:T(1024)S(1)} %bitcast.85, f32[1024,256]{1,0:T(8,128)S(1)} %fusion.132), kind=kCustom, calls=%fused_computation.9.clone.clone.1 | custom fusion | flops 262144 | bytes 3149824 | tf_op jit(solution)/shard_map/while/body/scatter-add | solution.py:142
  325.9 6.9 %collective-permute-done.56 = f32[256,256]{0,1:T(8,128)S(1)} collective-permute-done((f32[256,256]{0,1:T(8,128)S(1)}, f32[256,256]{0,1:T(8,128)S(1)}, u32[]{:S(2)}, u32[]{:S(2)}) %collective-permute-start.56) | collective-permute-done | bytes 262176 | tf_op jit(solution)/shard_map/ppermute | solution.py:25
  334.4 6.0 %collective-permute-done.57 = f32[256,256]{0,1:T(8,128)S(1)} collective-permute-done((f32[256,256]{0,1:T(8,128)S(1)}, f32[256,256]{0,1:T(8,128)S(1)}, u32[]{:S(2)}, u32[]{:S(2)}) %collective-permute-start.57) | collective-permute-done | bytes 262176 | tf_op jit(solution)/shard_map/ppermute | solution.py:25
  340.6 6.5 %collective-permute-done.58 = f32[256,256]{0,1:T(8,128)S(1)} collective-permute-done((f32[256,256]{0,1:T(8,128)S(1)}, f32[256,256]{0,1:T(8,128)S(1)}, u32[]{:S(2)}, u32[]{:S(2)}) %collective-permute-start.58) | collective-permute-done | bytes 262176 | tf_op jit(solution)/shard_map/ppermute | solution.py:25
  347.9 112.4 %all-reduce.5.cloned.1.call-done = f32[64,256]{1,0:T(8,128)} async-done(((f32[64,256]{1,0:T(8,128)}), f32[64,256]{1,0:T(8,128)}) %all-reduce.5.cloned.1.call-update) | async-done | bytes 65552 | tf_op jit(solution)/shard_map/psum | solution.py:166
  (264 shorter events, 101.2 us)
Async XLA Ops:
  7.2 286.0 %all-reduce.3.cloned.1.call-start = ((), (), s32[]{:S(2)}) async-start(), calls=%async_computation | async-start | bytes 131072 | tf_op jit(solution)/shard_map/psum | solution.py:166
  10.2 77.2 %collective-permute-start.10 = (bf16[256,256]{0,1:T(8,128)(2,1)S(1)}, bf16[256,256]{0,1:T(8,128)(2,1)S(1)}, u32[]{:S(2)}, u32[]{:S(2)}) collective-permute-start(bf16[256,256]{0,1:T(8,128)(2,1)S(1)} %select_convert_fusion.9), channel_id=1, source_target_pairs={{0,1},{1,0},{2,3},{3,2},{4,5},{5,4},{6,7},{7,6},{8,9},{9,8},{10,11... | collective-permute-start | bytes 393224 | tf_op jit(solution)/shard_map/ppermute | solution.py:25
  10.7 45.3 %collective-permute-start.15 = (s32[256]{0:T(256)S(1)}, s32[256]{0:T(256)S(1)}, u32[]{:S(2)}, u32[]{:S(2)}) collective-permute-start(s32[256]{0:T(256)S(1)} %bitcast.102), channel_id=1, source_target_pairs={{0,1},{1,0},{2,3},{3,2},{4,5},{5,4},{6,7},{7,6},{8,9},{9,8},{10,11... | collective-permute-start | bytes 3080 | tf_op jit(solution)/shard_map/ppermute | solution.py:25
  10.9 45.7 %collective-permute-start.5 = (s32[256]{0:T(256)S(1)}, s32[256]{0:T(256)S(1)}, u32[]{:S(2)}, u32[]{:S(2)}) collective-permute-start(s32[256]{0:T(256)S(1)} %bitcast.100), channel_id=1, source_target_pairs={{0,1},{1,0},{2,3},{3,2},{4,5},{5,4},{6,7},{7,6},{8,9},{9,8},{10,11... | collective-permute-start | bytes 3080 | tf_op jit(solution)/shard_map/ppermute | solution.py:25
  11.4 58.4 %collective-permute-start.20 = (s32[1024]{0:T(1024)S(1)}, s32[1024]{0:T(1024)S(1)}, u32[]{:S(2)}, u32[]{:S(2)}) collective-permute-start(s32[1024]{0:T(1024)S(1)} %bitcast.92), channel_id=1, source_target_pairs={{0,1},{1,0},{2,3},{3,2},{4,5},{5,4},{6,7},{7,6},{8,9},{9,8},{10,11... | collective-permute-start | bytes 12296 | tf_op jit(solution)/shard_map/ppermute | solution.py:25
  12.6 8.7 %collective-permute-start = (s32[1]{0:T(128)}, s32[1]{0:T(128)}, u32[]{:S(2)}, u32[]{:S(2)}) collective-permute-start(s32[1]{0:T(128)} %bitcast.10), channel_id=1, source_target_pairs={{0,1},{1,0},{2,3},{3,2},{4,5},{5,4},{6,7},{7,6},{8,9},{9,8},{10,11... | collective-permute-start | bytes 20 | tf_op jit(solution)/shard_map/ppermute | solution.py:25
  22.7 5.6 %collective-permute-start.1 = (s32[1]{0:T(128)}, s32[1]{0:T(128)}, u32[]{:S(2)}, u32[]{:S(2)}) collective-permute-start(s32[1]{0:T(128)} %select_n.511), channel_id=1, source_target_pairs={{0,2},{1,3},{2,0},{3,1},{4,6},{5,7},{6,4},{7,5},{8,10},{9,11},{10,... | collective-permute-start | bytes 20 | tf_op jit(solution)/shard_map/ppermute | solution.py:25
  56.6 81.8 %collective-permute-start.50 = (s32[1024]{0:T(1024)S(1)}, s32[1024]{0:T(1024)S(1)}, u32[]{:S(2)}, u32[]{:S(2)}) collective-permute-start(s32[1024]{0:T(1024)S(1)} %bitcast.90), channel_id=1, source_target_pairs={{0,1},{1,0},{2,3},{3,2},{4,5},{5,4},{6,7},{7,6},{8,9},{9,8},{10,11... | collective-permute-start | bytes 12296 | tf_op jit(solution)/shard_map/ppermute | solution.py:25
  67.4 59.6 %collective-permute-start.47 = (s32[256]{0:T(256)S(1)}, s32[256]{0:T(256)S(1)}, u32[]{:S(2)}, u32[]{:S(2)}) collective-permute-start(s32[256]{0:T(256)S(1)} %broadcast_select_fusion.32), channel_id=1, source_target_pairs={{0,4},{1,5},{2,6},{3,7},{4,0},{5,1},{6,2},{7,3},{8,12},{9,13},{10,... | collective-permute-start | bytes 3080 | tf_op jit(solution)/shard_map/ppermute | solution.py:25
  68.9 58.6 %collective-permute-start.37 = (s32[256]{0:T(256)S(1)}, s32[256]{0:T(256)S(1)}, u32[]{:S(2)}, u32[]{:S(2)}) collective-permute-start(s32[256]{0:T(256)S(1)} %broadcast_select_fusion.33), channel_id=1, source_target_pairs={{0,4},{1,5},{2,6},{3,7},{4,0},{5,1},{6,2},{7,3},{8,12},{9,13},{10,... | collective-permute-start | bytes 3080 | tf_op jit(solution)/shard_map/ppermute | solution.py:25
  87.5 5.0 %collective-permute-start.11 = (bf16[256,256]{0,1:T(8,128)(2,1)S(1)}, bf16[256,256]{0,1:T(8,128)(2,1)S(1)}, u32[]{:S(2)}, u32[]{:S(2)}) collective-permute-start(bf16[256,256]{0,1:T(8,128)(2,1)S(1)} %broadcast_select_fusion.11), channel_id=1, source_target_pairs={{0,2},{1,3},{2,0},{3,1},{4,6},{5,7},{6,4},{7,5},{8,10},{9,11},{10,... | collective-permute-start | bytes 393224 | tf_op jit(solution)/shard_map/ppermute | solution.py:25
  92.5 5.0 %collective-permute-start.12 = (bf16[256,256]{0,1:T(8,128)(2,1)S(1)}, bf16[256,256]{0,1:T(8,128)(2,1)S(1)}, u32[]{:S(2)}, u32[]{:S(2)}) collective-permute-start(bf16[256,256]{0,1:T(8,128)(2,1)S(1)} %broadcast_select_fusion.13), channel_id=1, source_target_pairs={{0,4},{1,5},{2,6},{3,7},{4,0},{5,1},{6,2},{7,3},{8,12},{9,13},{10,... | collective-permute-start | bytes 393224 | tf_op jit(solution)/shard_map/ppermute | solution.py:25
  93.5 5.7 %collective-permute-start.23 = (s32[1024]{0:T(1024)S(1)}, s32[1024]{0:T(1024)S(1)}, u32[]{:S(2)}, u32[]{:S(2)}) collective-permute-start(s32[1024]{0:T(1024)S(1)} %broadcast_select_fusion.27), channel_id=1, source_target_pairs={{0,8},{1,9},{2,10},{3,11},{4,12},{5,13},{6,14},{7,15},{8,0},{9,1},... | collective-permute-start | bytes 12296 | tf_op jit(solution)/shard_map/ppermute | solution.py:25
  99.2 5.9 %collective-permute-start.24 = (s32[1024]{0:T(1024)S(1)}, s32[1024]{0:T(1024)S(1)}, u32[]{:S(2)}, u32[]{:S(2)}) collective-permute-start(s32[1024]{0:T(1024)S(1)} %broadcast_select_fusion.28), channel_id=1, source_target_pairs={{0,16},{1,17},{2,18},{3,19},{4,20},{5,21},{6,22},{7,23},{8,24},{9,... | collective-permute-start | bytes 12296 | tf_op jit(solution)/shard_map/ppermute | solution.py:25
  102.7 7.3 %collective-permute-start.14 = (bf16[256,256]{0,1:T(8,128)(2,1)S(1)}, bf16[256,256]{0,1:T(8,128)(2,1)S(1)}, u32[]{:S(2)}, u32[]{:S(2)}) collective-permute-start(bf16[256,256]{0,1:T(8,128)(2,1)S(1)} %broadcast_select_fusion.17), channel_id=1, source_target_pairs={{0,16},{1,17},{2,18},{3,19},{4,20},{5,21},{6,22},{7,23},{8,24},{9,... | collective-permute-start | bytes 393224 | tf_op jit(solution)/shard_map/ppermute | solution.py:25
  129.3 8.1 %collective-permute-start.26 = (f32[256,256]{0,1:T(8,128)S(1)}, f32[256,256]{0,1:T(8,128)S(1)}, u32[]{:S(2)}, u32[]{:S(2)}) collective-permute-start(f32[256,256]{0,1:T(8,128)S(1)} %broadcast_select_fusion.10), channel_id=1, source_target_pairs={{0,2},{1,3},{2,0},{3,1},{4,6},{5,7},{6,4},{7,5},{8,10},{9,11},{10,... | collective-permute-start | bytes 786440 | tf_op jit(solution)/shard_map/ppermute | solution.py:25
  130.7 14.5 %collective-permute-start.49 = (s32[256]{0:T(256)S(1)}, s32[256]{0:T(256)S(1)}, u32[]{:S(2)}, u32[]{:S(2)}) collective-permute-start(s32[256]{0:T(256)S(1)} %broadcast_select_fusion.36), channel_id=1, source_target_pairs={{0,16},{1,17},{2,18},{3,19},{4,20},{5,21},{6,22},{7,23},{8,24},{9,... | collective-permute-start | bytes 3080 | tf_op jit(solution)/shard_map/ppermute | solution.py:25
  132.5 7.0 %collective-permute-start.39 = (s32[256]{0:T(256)S(1)}, s32[256]{0:T(256)S(1)}, u32[]{:S(2)}, u32[]{:S(2)}) collective-permute-start(s32[256]{0:T(256)S(1)} %broadcast_select_fusion.37), channel_id=1, source_target_pairs={{0,16},{1,17},{2,18},{3,19},{4,20},{5,21},{6,22},{7,23},{8,24},{9,... | collective-permute-start | bytes 3080 | tf_op jit(solution)/shard_map/ppermute | solution.py:25
  137.4 7.3 %collective-permute-start.27 = (f32[256,256]{0,1:T(8,128)S(1)}, f32[256,256]{0,1:T(8,128)S(1)}, u32[]{:S(2)}, u32[]{:S(2)}) collective-permute-start(f32[256,256]{0,1:T(8,128)S(1)} %broadcast_select_fusion.12), channel_id=1, source_target_pairs={{0,4},{1,5},{2,6},{3,7},{4,0},{5,1},{6,2},{7,3},{8,12},{9,13},{10,... | collective-permute-start | bytes 786440 | tf_op jit(solution)/shard_map/ppermute | solution.py:25
  138.3 16.6 %collective-permute-start.51 = (s32[1024]{0:T(1024)S(1)}, s32[1024]{0:T(1024)S(1)}, u32[]{:S(2)}, u32[]{:S(2)}) collective-permute-start(s32[1024]{0:T(1024)S(1)} %broadcast_select_fusion.20), channel_id=1, source_target_pairs={{0,2},{1,3},{2,0},{3,1},{4,6},{5,7},{6,4},{7,5},{8,10},{9,11},{10,... | collective-permute-start | bytes 12296 | tf_op jit(solution)/shard_map/ppermute | solution.py:25
  144.8 6.4 %collective-permute-start.28 = (f32[256,256]{0,1:T(8,128)S(1)}, f32[256,256]{0,1:T(8,128)S(1)}, u32[]{:S(2)}, u32[]{:S(2)}) collective-permute-start(f32[256,256]{0,1:T(8,128)S(1)} %broadcast_select_fusion.14), channel_id=1, source_target_pairs={{0,8},{1,9},{2,10},{3,11},{4,12},{5,13},{6,14},{7,15},{8,0},{9,1},... | collective-permute-start | bytes 786440 | tf_op jit(solution)/shard_map/ppermute | solution.py:25
  151.2 12.3 %collective-permute-start.29 = (f32[256,256]{0,1:T(8,128)S(1)}, f32[256,256]{0,1:T(8,128)S(1)}, u32[]{:S(2)}, u32[]{:S(2)}) collective-permute-start(f32[256,256]{0,1:T(8,128)S(1)} %broadcast_select_fusion.16), channel_id=1, source_target_pairs={{0,16},{1,17},{2,18},{3,19},{4,20},{5,21},{6,22},{7,23},{8,24},{9,... | collective-permute-start | bytes 786440 | tf_op jit(solution)/shard_map/ppermute | solution.py:25
  155.0 13.0 %collective-permute-start.52 = (s32[1024]{0:T(1024)S(1)}, s32[1024]{0:T(1024)S(1)}, u32[]{:S(2)}, u32[]{:S(2)}) collective-permute-start(s32[1024]{0:T(1024)S(1)} %broadcast_select_fusion.21), channel_id=1, source_target_pairs={{0,4},{1,5},{2,6},{3,7},{4,0},{5,1},{6,2},{7,3},{8,12},{9,13},{10,... | collective-permute-start | bytes 12296 | tf_op jit(solution)/shard_map/ppermute | solution.py:25
  169.3 5.6 %collective-permute-start.41 = (bf16[256,256]{0,1:T(8,128)(2,1)S(1)}, bf16[256,256]{0,1:T(8,128)(2,1)S(1)}, u32[]{:S(2)}, u32[]{:S(2)}) collective-permute-start(bf16[256,256]{0,1:T(8,128)(2,1)S(1)} %broadcast_select_fusion.1), channel_id=1, source_target_pairs={{0,2},{1,3},{2,0},{3,1},{4,6},{5,7},{6,4},{7,5},{8,10},{9,11},{10,... | collective-permute-start | bytes 393224 | tf_op jit(solution)/shard_map/ppermute | solution.py:25
  175.0 5.0 %collective-permute-start.42 = (bf16[256,256]{0,1:T(8,128)(2,1)S(1)}, bf16[256,256]{0,1:T(8,128)(2,1)S(1)}, u32[]{:S(2)}, u32[]{:S(2)}) collective-permute-start(bf16[256,256]{0,1:T(8,128)(2,1)S(1)} %broadcast_select_fusion.3), channel_id=1, source_target_pairs={{0,4},{1,5},{2,6},{3,7},{4,0},{5,1},{6,2},{7,3},{8,12},{9,13},{10,... | collective-permute-start | bytes 393224 | tf_op jit(solution)/shard_map/ppermute | solution.py:25
  176.2 284.1 %all-reduce.5.cloned.1.call-start = ((), (), s32[]{:S(2)}) async-start(), calls=%async_computation.1 | async-start | bytes 131072 | tf_op jit(solution)/shard_map/psum | solution.py:166
  180.0 114.6 %collective-permute-start.43 = (bf16[256,256]{0,1:T(8,128)(2,1)S(1)}, bf16[256,256]{0,1:T(8,128)(2,1)S(1)}, u32[]{:S(2)}, u32[]{:S(2)}) collective-permute-start(bf16[256,256]{0,1:T(8,128)(2,1)S(1)} %broadcast_select_fusion.5), channel_id=1, source_target_pairs={{0,8},{1,9},{2,10},{3,11},{4,12},{5,13},{6,14},{7,15},{8,0},{9,1},... | collective-permute-start | bytes 393224 | tf_op jit(solution)/shard_map/ppermute | solution.py:25
  294.7 10.2 %collective-permute-start.44 = (bf16[256,256]{0,1:T(8,128)(2,1)S(1)}, bf16[256,256]{0,1:T(8,128)(2,1)S(1)}, u32[]{:S(2)}, u32[]{:S(2)}) collective-permute-start(bf16[256,256]{0,1:T(8,128)(2,1)S(1)} %broadcast_select_fusion.7), channel_id=1, source_target_pairs={{0,16},{1,17},{2,18},{3,19},{4,20},{5,21},{6,22},{7,23},{8,24},{9,... | collective-permute-start | bytes 393224 | tf_op jit(solution)/shard_map/ppermute | solution.py:25
  324.4 8.4 %collective-permute-start.56 = (f32[256,256]{0,1:T(8,128)S(1)}, f32[256,256]{0,1:T(8,128)S(1)}, u32[]{:S(2)}, u32[]{:S(2)}) collective-permute-start(f32[256,256]{0,1:T(8,128)S(1)} %broadcast_select_fusion), channel_id=1, source_target_pairs={{0,2},{1,3},{2,0},{3,1},{4,6},{5,7},{6,4},{7,5},{8,10},{9,11},{10,... | collective-permute-start | bytes 786440 | tf_op jit(solution)/shard_map/ppermute | solution.py:25
  332.8 7.6 %collective-permute-start.57 = (f32[256,256]{0,1:T(8,128)S(1)}, f32[256,256]{0,1:T(8,128)S(1)}, u32[]{:S(2)}, u32[]{:S(2)}) collective-permute-start(f32[256,256]{0,1:T(8,128)S(1)} %broadcast_select_fusion.2), channel_id=1, source_target_pairs={{0,4},{1,5},{2,6},{3,7},{4,0},{5,1},{6,2},{7,3},{8,12},{9,13},{10,... | collective-permute-start | bytes 786440 | tf_op jit(solution)/shard_map/ppermute | solution.py:25
  340.4 6.7 %collective-permute-start.58 = (f32[256,256]{0,1:T(8,128)S(1)}, f32[256,256]{0,1:T(8,128)S(1)}, u32[]{:S(2)}, u32[]{:S(2)}) collective-permute-start(f32[256,256]{0,1:T(8,128)S(1)} %broadcast_select_fusion.4), channel_id=1, source_target_pairs={{0,8},{1,9},{2,10},{3,11},{4,12},{5,13},{6,14},{7,15},{8,0},{9,1},... | collective-permute-start | bytes 786440 | tf_op jit(solution)/shard_map/ppermute | solution.py:25
  347.1 114.7 %collective-permute-start.59 = (f32[256,256]{0,1:T(8,128)S(1)}, f32[256,256]{0,1:T(8,128)S(1)}, u32[]{:S(2)}, u32[]{:S(2)}) collective-permute-start(f32[256,256]{0,1:T(8,128)S(1)} %broadcast_select_fusion.6), channel_id=1, source_target_pairs={{0,16},{1,17},{2,18},{3,19},{4,20},{5,21},{6,22},{7,23},{8,24},{9,... | collective-permute-start | bytes 786440 | tf_op jit(solution)/shard_map/ppermute | solution.py:25
  (43 other events, 361.9 us)
Sparse Core Ops, SparseCore 0:
  176.3 116.7 all-reduce.2
  340.7 119.6 all-reduce.4
where the time goes:
time: 475 us; the launch traced here: 473 us
  waiting for transfers between devices  306 us (64%)
  starting transfers between devices  81.3 us (17%)
  between operations  29.2 us (6%)
  other arithmetic  29.1 us (6%)
  local copies, waits for them, and re-layouts  19.6 us (4%)
  matrix products  7.04 us (1%)
    psum x2, waiting for transfers between devices, on_device(): grad_total = lax.psum(grad_rel, 'dom')  225 us
    ppermute x60, waiting for transfers between devices, partner(): return lax.ppermute(value, axis, pairs)  81.3 us
    ppermute x60, starting transfers between devices, partner(): return lax.ppermute(value, axis, pairs)  81.2 us
    scatter-add x4, other arithmetic, group_step(): grad_local = grad_local.at[dst_in].add(grad_dst).at[neg_in].add(grad_neg)  16.9 us
  transfers between devices with their start and end apart: 62, of which 34 were waited for; matrix products, arithmetic and copies ran while one was open for 6% of the time, Pallas kernels for 0%

commit v1 on v0

v1 whole, which is shorter than its diff:
```python
import functools

import jax
import jax.numpy as jnp
from jax import lax
from jax.experimental import pallas as pl
from jax.experimental.pallas import tpu as pltpu
from jax.sharding import PartitionSpec as P

ROUNDS = 2
LANES = 128
LEARN_RATE = 0.1
EPSILON = 1e-06
DIGIT_BITS = 5
MAX_OWNERS = 16
MESH = pl.DeviceIdType.MESH
BF = jnp.bfloat16
F32 = jnp.float32


def digits_of(count):
    out, stride = [], 1
    while stride < count:
        size = min(2**DIGIT_BITS, count // stride)
        out.append((stride, size))
        stride *= size
    return out


def nt(a, b):
    return lax.dot_general(a, b, (((1,), (1,)), ((), ())), preferred_element_type=F32)


def nn(a, b):
    return lax.dot_general(a, b, (((1,), (0,)), ((), ())), preferred_element_type=F32)


def tn(a, b):
    return lax.dot_general(a, b, (((0,), (0,)), ((), ())), preferred_element_type=F32)


def split(x):
    high = x.astype(BF)
    return high, (x - high.astype(F32)).astype(BF)


def one_hot(row, size):
    place = lax.broadcasted_iota(jnp.int32, (size, row.shape[1]), 0)
    return jnp.where(place == row, 1.0, 0.0).astype(BF)


def identity_mask():
    shape = (LANES, LANES)
    return lax.broadcasted_iota(jnp.int32, shape, 0) == lax.broadcasted_iota(jnp.int32, shape, 1)


def to_column(rows):
    eye = identity_mask()
    parts = [
        jnp.sum(jnp.where(eye, rows[b : b + 1, :], 0.0), axis=1, keepdims=True)
        for b in range(rows.shape[0])
    ]
    return jnp.concatenate(parts, axis=0)


def to_rows(column):
    eye = identity_mask()
    parts = [
        jnp.sum(
            jnp.where(eye, column[b * LANES : (b + 1) * LANES, :], 0.0), axis=0, keepdims=True
        )
        for b in range(column.shape[0] // LANES)
    ]
    return jnp.concatenate(parts, axis=0)


def put_halves(ref, value):
    rows, columns = value.shape
    for b in range(columns // LANES):
        ref[b * rows : (b + 1) * rows, :] = value[:, b * LANES : (b + 1) * LANES]


def get_halves(ref, rows):
    value = ref[...]
    return jnp.concatenate(
        [value[b * rows : (b + 1) * rows] for b in range(value.shape[0] // rows)], axis=1
    )


def kernel(
    count,
    owners,
    matching,
    counts,
    emb_in,
    state_in,
    rel_in,
    rstate_in,
    src_index,
    dst_index,
    rel_index,
    neg_index,
    emb,
    state,
    rel,
    rstate,
    meta,
    pay,
    first,
    stage,
    second,
    local,
    embt,
    onehot,
    relg,
    parts,
    total,
    send_sem,
    recv_sem,
    meta_send,
    meta_recv,
    part_send,
    part_recv,
    total_send,
    total_recv,
):
    digits = digits_of(count)
    me = lax.axis_index("dom")
    rows_count, width = emb_in.shape
    half = width // 2
    rel_count = rel_in.shape[0]
    slots = src_index.shape[1]
    negs = neg_index.shape[1]
    idx_rows, hist_rows = slots // LANES, rows_count // LANES
    part_rows = relg.shape[1] // owners
    owner_stride = count // owners
    is_owner = lax.rem(me, owner_stride) == 0

    def other(step):
        return lax.rem(me + step, count)

    barrier = pltpu.get_barrier_semaphore()

    def greet(step, carry):
        pl.semaphore_signal(barrier, inc=1, device_id=(other(step),), device_id_type=MESH)
        return carry

    lax.fori_loop(1, count, greet, 0)

    def send(source, target, send_at, recv_at, device):
        pltpu.make_async_remote_copy(
            src_ref=source,
            dst_ref=target,
            send_sem=send_at,
            recv_sem=recv_at,
            device_id=(device,),
            device_id_type=MESH,
        ).start()

    def await_bytes(view, sem):
        pltpu.make_async_copy(view, view, sem).wait()

    def place(j):
        stride, size = digits[j]
        return stride, size, lax.rem(lax.div(me, stride), size)

    def exchange_out(k, way, j, source):
        stride, size, mine = place(j)
        rows = first[j][0].shape[1]

        def piece(there):
            return source.at[pl.ds(pl.multiple_of(there * rows, rows), rows)]

        first[j][k * 2 + way][mine] = piece(mine)[...]

        def step(t, carry):
            there = lax.rem(mine + t, size)
            send(
                piece(there),
                first[j][k * 2 + way].at[mine],
                send_sem.at[k, way, j, 0],
                recv_sem.at[k, way, j, 0],
                me + (there - mine) * stride,
            )
            return carry

        lax.fori_loop(1, size, step, 0)

    def exchange_on(k, way, j):
        stride, size, mine = place(j)
        rows = first[j][0].shape[1]
        mask = matching[k]
        if len(digits) > 1:
            mask = lax.rem(lax.div(mask, stride), size)
        here = pl.ds(pl.multiple_of(mine * rows, rows), rows)
        await_bytes(first[j][k * 2 + way].at[pl.ds(0, size - 1)], recv_sem.at[k, way, j, 0])

        def step(t, carry):
            there = lax.rem(mine + t, size)
            stage[j][k * 2 + way, there] = first[j][k * 2 + way][jnp.bitwise_xor(there, mask)]
            send(
                stage[j].at[k * 2 + way, there],
                second.at[k, way, j, here],
                send_sem.at[k, way, j, 1],
                recv_sem.at[k, way, j, 1],
                me + (there - mine) * stride,
            )
            return carry

        lax.fori_loop(1, size, step, 0)
        second[k, way, j, here, :] = first[j][k * 2 + way][jnp.bitwise_xor(mine, mask)]

    def exchange_in(k, way, j):
        _, size = digits[j]
        rows = first[j][0].shape[1]
        await_bytes(second.at[k, way, j, pl.ds(0, (size - 1) * rows)], recv_sem.at[k, way, j, 1])

    def exchange_rest(k, way):
        exchange_in(k, way, 0)
        for j in range(1, len(digits)):
            exchange_out(k, way, j, second.at[k, way, j - 1])
            exchange_on(k, way, j)
            exchange_in(k, way, j)

    def make_meta(k):
        number = lax.broadcasted_iota(jnp.int32, (1, slots), 1)
        marked = jnp.where(number < counts[k, 0], rel_index[k : k + 1, :], -1)
        negative = neg_index[k : k + 1, :]
        low = one_hot(jnp.bitwise_and(negative, LANES - 1), LANES)
        high = one_hot(jnp.right_shift(negative, 7), max(8, hist_rows))
        times = nt(high, low)[:hist_rows].astype(jnp.int32)
        dst = dst_index[k : k + 1, :]
        rows = [dst[:, b * LANES : (b + 1) * LANES] for b in range(idx_rows)]
        rows += [marked[:, b * LANES : (b + 1) * LANES] for b in range(idx_rows)]
        meta[k][me] = jnp.concatenate(rows + [times], axis=0)

    def send_meta(k):
        def step(t, carry):
            send(meta[k].at[me], meta[k].at[me], meta_send.at[k], meta_recv.at[k], other(t))
            return carry

        lax.fori_loop(1, count, step, 0)

    def gather_sources(k):
        values = emb_in[...] if k == 0 else emb[...]
        turned = values.T.astype(BF)
        embt[k] = turned
        chosen = one_hot(src_index[k : k + 1, :], rows_count)
        onehot[k] = chosen
        put_halves(pay.at[k, 0], nn(turned, chosen).astype(BF))

    def work(k):
        relations = rel_in[...] if k == 0 else rel[...]
        values = (emb_in[...] if k == 0 else emb[...]).astype(BF)
        source = get_halves(second.at[k, 0, len(digits) - 1], width).astype(F32)
        await_bytes(meta[k].at[pl.ds(0, count - 1)], meta_recv.at[k])
        info = meta[k][jnp.bitwise_xor(me, matching[k])]
        dst_row = jnp.concatenate([info[b : b + 1] for b in range(idx_rows)], axis=1)
        rel_row = jnp.concatenate(
            [info[b : b + 1] for b in range(idx_rows, 2 * idx_rows)], axis=1
        )
        times = to_column(info[2 * idx_rows : 2 * idx_rows + hist_rows].astype(F32))
        live = jnp.where(rel_row >= 0, 1.0, 0.0)
        dst_hot = one_hot(dst_row, rows_count)
        rel_hot = one_hot(rel_row, rel_count)
        target = nn(embt[k], dst_hot)
        rel_high, rel_low = split(relations)
        factor = tn(rel_high, rel_hot) + tn(rel_low, rel_hot)
        s_re, s_im = source[:half], source[half:]
        r_re, r_im = factor[:half], factor[half:]
        query = jnp.concatenate([s_re * r_re - s_im * r_im, s_re * r_im + s_im * r_re], axis=0)
        positive = jnp.sum(query * target, axis=0, keepdims=True)
        query_b = query.astype(BF)
        scores = nn(values, query_b)
        weights = (jax.nn.sigmoid(scores) * (times * (1.0 / negs)) * live).astype(BF)
        grad_pos = -jax.nn.sigmoid(-positive) * live
        grad_query = grad_pos * target + nn(embt[k], weights)
        g_re, g_im = grad_query[:half], grad_query[half:]
        put_halves(
            pay.at[k, 1],
            jnp.concatenate([g_re * r_re + g_im * r_im, g_im * r_re - g_re * r_im], axis=0).astype(
                BF
            ),
        )
        exchange_out(k, 1, 0, pay.at[k, 1])
        rel_high, rel_low = split(
            jnp.concatenate([g_re * s_re + g_im * s_im, g_im * s_re - g_re * s_im], axis=0)
        )
        put_halves(relg.at[k], nt(rel_hot, rel_high) + nt(rel_hot, rel_low))
        send_parts(k)
        dst_high, dst_low = split(grad_pos * query)
        local[...] = nt(weights, query_b) + nt(dst_hot, dst_high) + nt(dst_hot, dst_low)

    my_part = pl.ds(pl.multiple_of(me * part_rows, part_rows), part_rows)
    owner = lax.div(me, owner_stride)
    owned = pl.ds(pl.multiple_of(owner * part_rows, part_rows), part_rows)

    def send_parts(k):
        def step(o, carry):
            device = o * owner_stride

            @pl.when(device != me)
            def _():
                send(
                    relg.at[k, pl.ds(pl.multiple_of(o * part_rows, part_rows), part_rows)],
                    parts.at[k, my_part],
                    part_send.at[k],
                    part_recv.at[k],
                    device,
                )

            return carry

        lax.fori_loop(0, owners, step, 0)

        @pl.when(is_owner)
        def _():
            parts[k, my_part, :] = relg[k, owned, :]

    def add_parts(k):
        @pl.when(is_owner)
        def _():
            await_bytes(parts.at[k, pl.ds(0, (count - 1) * part_rows)], part_recv.at[k])
            added = parts[k].reshape(count, part_rows, LANES)
            total[k, owned, :] = jnp.sum(added, axis=0)

            def step(t, carry):
                send(
                    total.at[k, owned],
                    total.at[k, owned],
                    total_send.at[k],
                    total_recv.at[k],
                    other(t),
                )
                return carry

            lax.fori_loop(1, count, step, 0)

    def update_relations(k):
        @pl.when(is_owner)
        def _():
            await_bytes(total.at[k, pl.ds(0, (owners - 1) * part_rows)], total_recv.at[k])

        if owners < count:

            @pl.when(jnp.logical_not(is_owner))
            def _():
                await_bytes(total.at[k], total_recv.at[k])

        grad = get_halves(total.at[k], rel_count)
        new_state = (rstate_in[...] if k == 0 else rstate[...]) + grad * grad
        rstate[...] = new_state
        rel[...] = (rel_in[...] if k == 0 else rel[...]) - LEARN_RATE * grad / (
            jnp.sqrt(new_state) + EPSILON
        )

    def update_entities(k):
        returned = get_halves(second.at[k, 1, len(digits) - 1], width)
        grad = local[...] + nt(onehot[k], returned)
        old_state = to_column(state_in[...] if k == 0 else state[...])
        new_state = old_state + jnp.sum(grad * grad, axis=1, keepdims=True) * (1.0 / width)
        state[...] = to_rows(new_state)
        emb[...] = (emb_in[...] if k == 0 else emb[...]) - grad * (
            LEARN_RATE / (jnp.sqrt(new_state) + EPSILON)
        )

    gather_sources(0)
    make_meta(0)
    pl.semaphore_wait(barrier, count - 1)
    exchange_out(0, 0, 0, pay.at[0, 0])
    send_meta(0)
    for k in range(ROUNDS):
        exchange_on(k, 0, 0)
        if k + 1 < ROUNDS:
            make_meta(k + 1)
        if k > 0:
            update_relations(k - 1)
        exchange_rest(k, 0)
        work(k)
        exchange_on(k, 1, 0)
        if k + 1 < ROUNDS:
            send_meta(k + 1)
        add_parts(k)
        exchange_rest(k, 1)
        update_entities(k)
        if k + 1 < ROUNDS:
            gather_sources(k + 1)
            exchange_out(k + 1, 0, 0, pay.at[k + 1, 0])
    update_relations(ROUNDS - 1)

    for k in range(ROUNDS):
        for way in range(2):
            for j in range(len(digits)):
                _, size = digits[j]
                for phase in range(2):
                    view = stage[j].at[k * 2 + way, pl.ds(0, size - 1)]
                    await_bytes(view, send_sem.at[k, way, j, phase])
        await_bytes(meta[k].at[pl.ds(0, count - 1)], meta_send.at[k])

        @pl.when(is_owner)
        def _():
            await_bytes(relg.at[k, pl.ds(0, (owners - 1) * part_rows)], part_send.at[k])
            await_bytes(parts.at[k, pl.ds(0, (count - 1) * part_rows)], total_send.at[k])

        if owners < count:

            @pl.when(jnp.logical_not(is_owner))
            def _():
                await_bytes(relg.at[k], part_send.at[k])


def on_device(count, embeddings, emb_state, relations, rel_state, matching, *lists):
    src_index, dst_index, rel_index, neg_index, counts = lists
    rows_count, width = embeddings.shape
    slots = src_index.shape[1]
    rel_count = relations.shape[0]
    digits = len(digits_of(count))
    owners = min(MAX_OWNERS, count)
    pay_rows = width * (slots // LANES)
    meta_rows = 2 * (slots // LANES) + rows_count // LANES
    rel_rows = rel_count * (width // LANES)
    vmem, smem = (pl.BlockSpec(memory_space=space) for space in (pltpu.VMEM, pltpu.SMEM))
    dma = pltpu.SemaphoreType.DMA
    pieces = tuple(
        pltpu.VMEM((ROUNDS * 2, size, pay_rows // size, LANES), BF)
        for _, size in digits_of(count)
    )
    arriving = tuple(
        (pltpu.VMEM((size, pay_rows // size, LANES), BF),) * (ROUNDS * 2)
        for _, size in digits_of(count)
    )
    out = pl.pallas_call(
        functools.partial(kernel, count, owners),
        out_shape=(
            jax.ShapeDtypeStruct((rows_count, width), F32),
            jax.ShapeDtypeStruct((rows_count // LANES, LANES), F32),
            jax.ShapeDtypeStruct((rel_count, width), F32),
            jax.ShapeDtypeStruct((rel_count, width), F32),
        ),
        in_specs=[smem, smem] + [vmem] * 8,
        out_specs=(vmem,) * 4,
        scratch_shapes=[
            (pltpu.VMEM((count, meta_rows, LANES), jnp.int32),) * ROUNDS,
            pltpu.VMEM((ROUNDS, 2, pay_rows, LANES), BF),
            arriving,
            pieces,
            pltpu.VMEM((ROUNDS, 2, digits, pay_rows, LANES), BF),
            pltpu.VMEM((rows_count, width), F32),
            pltpu.VMEM((ROUNDS, width, rows_count), BF),
            pltpu.VMEM((ROUNDS, rows_count, slots), BF),
            pltpu.VMEM((ROUNDS, rel_rows, LANES), F32),
            pltpu.VMEM((ROUNDS, count * (rel_rows // owners), LANES), F32),
            pltpu.VMEM((ROUNDS, rel_rows, LANES), F32),
            dma((ROUNDS, 2, digits, 2)),
            dma((ROUNDS, 2, digits, 2)),
            dma((ROUNDS,)),
            dma((ROUNDS,)),
            dma((ROUNDS,)),
            dma((ROUNDS,)),
            dma((ROUNDS,)),
            dma((ROUNDS,)),
        ],
        compiler_params=pltpu.CompilerParams(
            collective_id=0, has_side_effects=True, vmem_limit_bytes=40 * 2**20
        ),
    )(
        matching,
        counts,
        embeddings,
        emb_state.reshape(rows_count // LANES, LANES),
        relations,
        rel_state,
        src_index,
        dst_index,
        rel_index,
        neg_index,
    )
    return out[0], out[1].reshape(rows_count), out[2], out[3]


def solution(mesh):
    return jax.shard_map(
        functools.partial(on_device, mesh.shape["dom"]),
        mesh=mesh,
        in_specs=(
            P("dom", None),
            P("dom"),
            P(),
            P(),
            P(),
            P(None, "dom"),
            P(None, "dom"),
            P(None, "dom"),
            P(None, "dom"),
            P(None, "dom"),
        ),
        out_specs=(P("dom", None), P("dom"), P(), P()),
        check_vma=False,
    )
```

time: 475 us -> 69.4 us (0.15)
  waiting for transfers between devices: 306 us -> 0 us
  starting transfers between devices: 81.3 us -> 0 us
  Pallas kernels: 0 us -> 58.9 us
  other arithmetic: 29.1 us -> 0 us
  between operations: 29.2 us -> 0.67 us
  local copies, waits for them, and re-layouts: 19.6 us -> 9.38 us
  matrix products: 7.04 us -> 0 us
    psum x2 -> x0, waiting for transfers between devices: 225 us -> none  [on_device(): grad_total = lax.psum(grad_rel, 'dom')]
    ppermute x60 -> x0, waiting for transfers between devices: 81.3 us -> none  [partner(): return lax.ppermute(value, axis, pairs)]
    ppermute x60 -> x0, starting transfers between devices: 81.2 us -> none  [partner(): return lax.ppermute(value, axis, pairs)]
    pallas_call x0 -> x1, Pallas kernels: none -> 58.9 us  [on_device(): pl.pallas_call(functools.partial(kernel, count, owners), out_shape=(jax.S...]
    scatter-add x6 -> x0, other arithmetic: 21.2 us -> none  [the longest x4 16.9 us: group_step(): grad_local = grad_local.at[dst_in].add(grad_dst).at[neg_in].add(grad_neg)]
    gather x10 -> x0, local copies, waits for them, and re-layouts: 13.2 us -> none  [the longest x2 7.88 us: group_step(): neg_bf = jnp.take(embeddings, neg_in, axis=0).astype(jnp.bfloat16)]
    dot_general x12 -> x0, matrix products: 7.04 us -> none  [the longest x4 3.11 us: group_step(): jnp.dot(selector, relations, precision=lax.Precision.HIGHEST, preferred_e...]
    unnamed x26 -> x25, local copies, waits for them, and re-layouts: 2.39 us -> 9.38 us
  transfers between devices with their start and end apart: 62 -> 0, of which waited for: 34 -> 0; matrix products, arithmetic and copies ran while one was open for 6% -> 0% of each run, Pallas kernels for 0% -> 0%
where the time goes in v1:
time: 69.4 us; the launch traced here: 69 us
  Pallas kernels  58.9 us (85%)
  local copies, waits for them, and re-layouts  9.38 us (14%)
    pallas_call x1, Pallas kernels, on_device(): pl.pallas_call(functools.partial(kernel, count, owners), out_shape=(jax.S...  58.9 us
    unnamed x25, local copies, waits for them, and re-layouts  9.38 us

profile of v1, /device:TPU:0, one launch (start us, length us, event | category | flops | bytes accessed | tf_op | source)
XLA Modules:
  0.0 69.0 jit_solution(4066482036809558921)
XLA Ops:
  0.6 0.0 copy-start.9
  0.6 0.0 copy-start.4
  0.7 0.6 copy-done.9
  1.3 0.0 copy-start.8
  1.3 0.1 copy.14.counts
  1.4 0.0 copy-done.4
  1.4 0.6 copy-done.8
  1.9 0.0 copy-start
  1.9 1.0 %copy-done = f32[512,256]{1,0:T(8,128)S(1)} copy-done((f32[512,256]{1,0:T(8,128)S(1)}, f32[512,256]{1,0:T(8,128)}, u32[]{:S(2)}) %copy-start) | copy-done | bytes 524312
  3.0 0.0 copy-start.1
  3.0 0.8 %copy-done.1 = f32[64,256]{1,0:T(8,128)S(1)} copy-done((f32[64,256]{1,0:T(8,128)S(1)}, f32[64,256]{1,0:T(8,128)}, u32[]{:S(2)}) %copy-start.1) | copy-done | bytes 65560
  3.8 0.0 copy-start.2
  3.8 0.8 %copy-done.2 = f32[64,256]{1,0:T(8,128)S(1)} copy-done((f32[64,256]{1,0:T(8,128)S(1)}, f32[64,256]{1,0:T(8,128)}, u32[]{:S(2)}) %copy-start.2) | copy-done | bytes 65560
  4.7 0.0 copy-start.3
  4.7 0.7 %copy-done.3 = s32[2,1024]{1,0:T(2,128)S(1)} copy-done((s32[2,1024]{1,0:T(2,128)S(1)}, s32[2,1024]{1,0:T(2,128)}, u32[]{:S(2)}) %copy-start.3) | copy-done | bytes 8216
  5.4 0.0 copy-start.5
  5.4 0.7 copy-done.5
  6.0 0.0 copy-start.6
  6.0 0.7 copy-done.6
  6.7 0.0 copy-start.7
  6.7 0.7 copy-done.7
  7.4 58.9 %shard_map.129 = (f32[512,256]{1,0:T(8,128)S(1)}, f32[4,128]{1,0:T(4,128)S(1)}, f32[64,256]{1,0:T(8,128)S(1)}, f32[64,256]{1,0:T(8,128)S(1)}) custom-call(s32[2]{0:T(128)S(1)} %copy-done.8, s32[2,1]{1,0:T(2,128)S(1)} %copy.14.counts, f32[512,256]{1,0:T(8,128)S(1)} %copy-done, f32[4,128]{1,0:T(4,128)S(1)} %bitcast.2, f32[64,256]{1,0:T(8,128)S(1)} %copy-done.1, ...), custom_call_target="tpu_custom_call" | custom-call | tf_op jit(solution)/shard_map/pallas_call | solution.py:432
  66.4 0.8 %copy.19 = f32[512,256]{1,0:T(8,128)} copy(f32[512,256]{1,0:T(8,128)S(1)} %get-tuple-element.16) | data formatting | bytes 1048576
  67.2 0.6 copy.20
  67.7 0.6 copy.21
  68.4 0.6 copy.22
Async XLA Ops:
  0.6 0.7 copy-start.9
  0.6 0.7 %copy-start.4 = (f32[512]{0:T(512)S(1)}, f32[512]{0:T(512)}, u32[]{:S(2)}) copy-start(f32[512]{0:T(512)} %param.11) | copy-start | bytes 6148
  1.3 0.7 copy-start.8
  1.9 1.0 %copy-start = (f32[512,256]{1,0:T(8,128)S(1)}, f32[512,256]{1,0:T(8,128)}, u32[]{:S(2)}) copy-start(f32[512,256]{1,0:T(8,128)} %emb_in.1) | copy-start | bytes 1572868
  3.0 0.8 %copy-start.1 = (f32[64,256]{1,0:T(8,128)S(1)}, f32[64,256]{1,0:T(8,128)}, u32[]{:S(2)}) copy-start(f32[64,256]{1,0:T(8,128)} %rel_in.1) | copy-start | bytes 196612
  3.8 0.8 %copy-start.2 = (f32[64,256]{1,0:T(8,128)S(1)}, f32[64,256]{1,0:T(8,128)}, u32[]{:S(2)}) copy-start(f32[64,256]{1,0:T(8,128)} %rstate_in.1) | copy-start | bytes 196612
  4.7 0.7 %copy-start.3 = (s32[2,1024]{1,0:T(2,128)S(1)}, s32[2,1024]{1,0:T(2,128)}, u32[]{:S(2)}) copy-start(s32[2,1024]{1,0:T(2,128)} %neg_index.1) | copy-start | bytes 24580
  5.4 0.7 copy-start.5
  6.0 0.7 copy-start.6
  6.7 0.7 copy-start.7

commit v2 on v1

--- a/solution.py
+++ b/solution.py
@@ -92,6 +92,18 @@
     owners,
     matching,
     counts,
+    emb_arg,
+    state_arg,
+    rel_arg,
+    rstate_arg,
+    src_arg,
+    dst_arg,
+    rel_index_arg,
+    neg_arg,
+    emb,
+    state,
+    rel,
+    rstate,
     emb_in,
     state_in,
     rel_in,
@@ -100,10 +112,6 @@
     dst_index,
     rel_index,
     neg_index,
-    emb,
-    state,
-    rel,
-    rstate,
     meta,
     pay,
     first,
@@ -123,7 +131,25 @@
     part_recv,
     total_send,
     total_recv,
+    load_sem,
 ):
+    loads = [
+        pltpu.make_async_copy(source, target, load_sem.at[i])
+        for i, (source, target) in enumerate(
+            (
+                (emb_arg, emb_in),
+                (src_arg, src_index),
+                (neg_arg, neg_index),
+                (dst_arg, dst_index),
+                (rel_index_arg, rel_index),
+                (state_arg, state_in),
+                (rel_arg, rel_in),
+                (rstate_arg, rstate_in),
+            )
+        )
+    ]
+    for load in loads:
+        load.start()
     digits = digits_of(count)
     me = lax.axis_index("dom")
     rows_count, width = emb_in.shape
@@ -224,7 +250,7 @@
 
     def make_meta(k):
         number = lax.broadcasted_iota(jnp.int32, (1, slots), 1)
-        marked = jnp.where(number < counts[k, 0], rel_index[k : k + 1, :], -1)
+        marked = jnp.where(number < counts[k], rel_index[k : k + 1, :], -1)
         negative = neg_index[k : k + 1, :]
         low = one_hot(jnp.bitwise_and(negative, LANES - 1), LANES)
         high = one_hot(jnp.right_shift(negative, 7), max(8, hist_rows))
@@ -364,7 +390,11 @@
             LEARN_RATE / (jnp.sqrt(new_state) + EPSILON)
         )
 
+    loads[0].wait()
+    loads[1].wait()
     gather_sources(0)
+    for load in loads[2:]:
+        load.wait()
     make_meta(0)
     pl.semaphore_wait(barrier, count - 1)
     exchange_out(0, 0, 0, pay.at[0, 0])
@@ -407,6 +437,14 @@
             @pl.when(jnp.logical_not(is_owner))
             def _():
                 await_bytes(relg.at[k], part_send.at[k])
+
+
+def store(*refs):
+    copies = [pltpu.make_async_copy(refs[i], refs[4 + i], refs[8].at[i]) for i in range(4)]
+    for copy in copies:
+        copy.start()
+    for copy in copies:
+        copy.wait()
 
 
 def on_device(count, embeddings, emb_state, relations, rel_state, matching, *lists):
@@ -437,9 +475,17 @@
             jax.ShapeDtypeStruct((rel_count, width), F32),
             jax.ShapeDtypeStruct((rel_count, width), F32),
         ),
-        in_specs=[smem, smem] + [vmem] * 8,
+        in_specs=[smem, smem] + [pl.BlockSpec(memory_space=pltpu.HBM)] * 8,
         out_specs=(vmem,) * 4,
         scratch_shapes=[
+            pltpu.VMEM((rows_count, width), F32),
+            pltpu.VMEM((rows_count // LANES, LANES), F32),
+            pltpu.VMEM((rel_count, width), F32),
+            pltpu.VMEM((rel_count, width), F32),
+            pltpu.VMEM(src_index.shape, jnp.int32),
+            pltpu.VMEM(dst_index.shape, jnp.int32),
+            pltpu.VMEM(rel_index.shape, jnp.int32),
+            pltpu.VMEM(neg_index.shape, jnp.int32),
             (pltpu.VMEM((count, meta_rows, LANES), jnp.int32),) * ROUNDS,
             pltpu.VMEM((ROUNDS, 2, pay_rows, LANES), BF),
             arriving,
@@ -459,13 +505,14 @@
             dma((ROUNDS,)),
             dma((ROUNDS,)),
             dma((ROUNDS,)),
+            dma((8,)),
         ],
         compiler_params=pltpu.CompilerParams(
-            collective_id=0, has_side_effects=True, vmem_limit_bytes=40 * 2**20
+            collective_id=0, has_side_effects=True, vmem_limit_bytes=62 * 2**20
         ),
     )(
         matching,
-        counts,
+        counts.reshape(ROUNDS),
         embeddings,
         emb_state.reshape(rows_count // LANES, LANES),
         relations,
@@ -475,6 +522,13 @@
         rel_index,
         neg_index,
     )
+    out = pl.pallas_call(
+        store,
+        out_shape=tuple(jax.ShapeDtypeStruct(x.shape, x.dtype) for x in out),
+        in_specs=[vmem] * 4,
+        out_specs=(pl.BlockSpec(memory_space=pltpu.HBM),) * 4,
+        scratch_shapes=[dma((4,))],
+    )(*out)
     return out[0], out[1].reshape(rows_count), out[2], out[3]
 
 

time: 69.4 us -> 62.7 us (0.903)
  local copies, waits for them, and re-layouts: 9.38 us -> 0 us
  Pallas kernels: 58.9 us -> 61.9 us
    unnamed x25 -> x0, local copies, waits for them, and re-layouts: 9.38 us -> none
    pallas_call x0 -> x1, Pallas kernels: none -> 1.91 us  [on_device(): pl.pallas_call(store, out_shape=tuple((jax.ShapeDtypeStruct(x.shape, x.dt...]
    pallas_call x1, Pallas kernels: 58.9 us -> 60 us  [on_device(): pl.pallas_call(functools.partial(kernel, count, owners), out_shape=(jax.S...]
where the time goes in v2:
time: 62.7 us; the launch traced here: 62.5 us
  Pallas kernels  61.9 us (99%)
  between operations  0.64 us (1%)
    pallas_call x1, Pallas kernels, on_device(): pl.pallas_call(functools.partial(kernel, count, owners), out_shape=(jax.S...  60 us
    pallas_call x1, Pallas kernels, on_device(): pl.pallas_call(store, out_shape=tuple((jax.ShapeDtypeStruct(x.shape, x.dt...  1.91 us

profile of v2, /device:TPU:0, one launch (start us, length us, event | category | flops | bytes accessed | tf_op | source)
XLA Modules:
  0.0 62.5 jit_solution(17818234781620279408)
XLA Ops:
  0.6 60.0 %shard_map.129 = (f32[512,256]{1,0:T(8,128)}, f32[4,128]{1,0:T(4,128)}, f32[64,256]{1,0:T(8,128)}, f32[64,256]{1,0:T(8,128)}) custom-call(s32[2]{0:T(128)} %matching.1, s32[2]{0:T(128)} %bitcast.4, f32[512,256]{1,0:T(8,128)} %emb_arg.1, f32[4,128]{1,0:T(4,128)} %bitcast.3, f32[64,256]{1,0:T(8,128)} %rel_arg.1, f32[64,256]{1,0:T(8,128)} %rstate_arg.1, ...), custom_call_target="tpu_custom_call" | custom-call | tf_op jit(solution)/shard_map/pallas_call | solution.py:470
  60.6 1.9 %shard_map.130 = (f32[512,256]{1,0:T(8,128)}, f32[4,128]{1,0:T(4,128)}, f32[64,256]{1,0:T(8,128)}, f32[64,256]{1,0:T(8,128)}) custom-call(f32[512,256]{1,0:T(8,128)} %get-tuple-element.12.refs_0_, f32[4,128]{1,0:T(4,128)} %get-tuple-element.13.refs_1_, f32[64,256]{1,0:T(8,128)} %get-tuple-element.14.refs_2_, f32[64,256]{1,0:T(8,128)} %get-tuple-element.15.refs_3_), custom_call_target="tpu_custom_call" | custom-call | tf_op jit(solution)/shard_map/pallas_call | solution.py:525

commit v3 on v2

--- a/solution.py
+++ b/solution.py
@@ -267,18 +267,17 @@
 
         lax.fori_loop(1, count, step, 0)
 
+    def choose(k):
+        onehot[k] = one_hot(src_index[k : k + 1, :], rows_count)
+
     def gather_sources(k):
         values = emb_in[...] if k == 0 else emb[...]
-        turned = values.T.astype(BF)
+        turned = values.astype(BF).T
         embt[k] = turned
-        chosen = one_hot(src_index[k : k + 1, :], rows_count)
-        onehot[k] = chosen
-        put_halves(pay.at[k, 0], nn(turned, chosen).astype(BF))
-
-    def work(k):
+        put_halves(pay.at[k, 0], nn(turned, onehot[k]).astype(BF))
+
+    def prepare(k):
         relations = rel_in[...] if k == 0 else rel[...]
-        values = (emb_in[...] if k == 0 else emb[...]).astype(BF)
-        source = get_halves(second.at[k, 0, len(digits) - 1], width).astype(F32)
         await_bytes(meta[k].at[pl.ds(0, count - 1)], meta_recv.at[k])
         info = meta[k][jnp.bitwise_xor(me, matching[k])]
         dst_row = jnp.concatenate([info[b : b + 1] for b in range(idx_rows)], axis=1)
@@ -292,13 +291,18 @@
         target = nn(embt[k], dst_hot)
         rel_high, rel_low = split(relations)
         factor = tn(rel_high, rel_hot) + tn(rel_low, rel_hot)
+        return target, factor, live, times * (1.0 / negs), dst_hot, rel_hot
+
+    def work(k, target, factor, live, times, dst_hot, rel_hot):
+        values = (emb_in[...] if k == 0 else emb[...]).astype(BF)
+        source = get_halves(second.at[k, 0, len(digits) - 1], width).astype(F32)
         s_re, s_im = source[:half], source[half:]
         r_re, r_im = factor[:half], factor[half:]
         query = jnp.concatenate([s_re * r_re - s_im * r_im, s_re * r_im + s_im * r_re], axis=0)
         positive = jnp.sum(query * target, axis=0, keepdims=True)
         query_b = query.astype(BF)
         scores = nn(values, query_b)
-        weights = (jax.nn.sigmoid(scores) * (times * (1.0 / negs)) * live).astype(BF)
+        weights = (jax.nn.sigmoid(scores) * times * live).astype(BF)
         grad_pos = -jax.nn.sigmoid(-positive) * live
         grad_query = grad_pos * target + nn(embt[k], weights)
         g_re, g_im = grad_query[:half], grad_query[half:]
@@ -380,10 +384,9 @@
             jnp.sqrt(new_state) + EPSILON
         )
 
-    def update_entities(k):
+    def update_entities(k, old_state):
         returned = get_halves(second.at[k, 1, len(digits) - 1], width)
         grad = local[...] + nt(onehot[k], returned)
-        old_state = to_column(state_in[...] if k == 0 else state[...])
         new_state = old_state + jnp.sum(grad * grad, axis=1, keepdims=True) * (1.0 / width)
         state[...] = to_rows(new_state)
         emb[...] = (emb_in[...] if k == 0 else emb[...]) - grad * (
@@ -392,6 +395,7 @@
 
     loads[0].wait()
     loads[1].wait()
+    choose(0)
     gather_sources(0)
     for load in loads[2:]:
         load.wait()
@@ -403,16 +407,19 @@
         exchange_on(k, 0, 0)
         if k + 1 < ROUNDS:
             make_meta(k + 1)
+            choose(k + 1)
         if k > 0:
             update_relations(k - 1)
+        ready = prepare(k)
         exchange_rest(k, 0)
-        work(k)
+        work(k, *ready)
         exchange_on(k, 1, 0)
         if k + 1 < ROUNDS:
             send_meta(k + 1)
         add_parts(k)
+        old_state = to_column(state_in[...] if k == 0 else state[...])
         exchange_rest(k, 1)
-        update_entities(k)
+        update_entities(k, old_state)
         if k + 1 < ROUNDS:
             gather_sources(k + 1)
             exchange_out(k + 1, 0, 0, pay.at[k + 1, 0])

time: 62.7 us -> 61.8 us (0.986)
  Pallas kernels: 61.9 us -> 61 us
    pallas_call x1, Pallas kernels: 60 us -> 59.1 us  [on_device(): pl.pallas_call(functools.partial(kernel, count, owners), out_shape=(jax.S...]
where the time goes in v3:
time: 61.8 us; the launch traced here: 61.6 us
  Pallas kernels  61 us (99%)
  between operations  0.64 us (1%)
    pallas_call x1, Pallas kernels, on_device(): pl.pallas_call(functools.partial(kernel, count, owners), out_shape=(jax.S...  59.1 us
    pallas_call x1, Pallas kernels, on_device(): pl.pallas_call(store, out_shape=tuple((jax.ShapeDtypeStruct(x.shape, x.dt...  1.91 us

profile of v3, /device:TPU:0, one launch (start us, length us, event | category | flops | bytes accessed | tf_op | source)
XLA Modules:
  0.0 61.6 jit_solution(7407950987554686388)
XLA Ops:
  0.6 59.1 %shard_map.129 = (f32[512,256]{1,0:T(8,128)}, f32[4,128]{1,0:T(4,128)}, f32[64,256]{1,0:T(8,128)}, f32[64,256]{1,0:T(8,128)}) custom-call(s32[2]{0:T(128)} %matching.1, s32[2]{0:T(128)} %bitcast.4, f32[512,256]{1,0:T(8,128)} %emb_arg.1, f32[4,128]{1,0:T(4,128)} %bitcast.3, f32[64,256]{1,0:T(8,128)} %rel_arg.1, f32[64,256]{1,0:T(8,128)} %rstate_arg.1, ...), custom_call_target="tpu_custom_call" | custom-call | tf_op jit(solution)/shard_map/pallas_call | solution.py:477
  59.7 1.9 %shard_map.130 = (f32[512,256]{1,0:T(8,128)}, f32[4,128]{1,0:T(4,128)}, f32[64,256]{1,0:T(8,128)}, f32[64,256]{1,0:T(8,128)}) custom-call(f32[512,256]{1,0:T(8,128)} %get-tuple-element.12.refs_0_, f32[4,128]{1,0:T(4,128)} %get-tuple-element.13.refs_1_, f32[64,256]{1,0:T(8,128)} %get-tuple-element.14.refs_2_, f32[64,256]{1,0:T(8,128)} %get-tuple-element.15.refs_3_), custom_call_target="tpu_custom_call" | custom-call | tf_op jit(solution)/shard_map/pallas_call | solution.py:532
